TPU v7x, 256 devices: a whole 4x4x8 slice. The times are simulated.
256 devices in a mesh: ep: 8 (over z_hi, x), fsdp: 32 (over y, z_lo, core).
Axes of the slice: x: 4, y: 4, z: 8 (z_hi: 2, z_lo: 4; z = z_hi * 4 + z_lo), core: 2. Of those that a mesh axis runs over, the one named last changes fastest.
Arguments:
- tokens: bfloat16 [1024, 6144], P('ep', 'fsdp'), may hold values from -6 to 6
- expert_ids: int32 [1024, 2], P('ep'), may hold values from 0 to 7, all different within a row; in each aligned block of 128 rows (0 to 127, 128 to 255, ...) at most 64 rows name the same one
- combine_weights: float32 [1024, 2], P('ep'), may hold values from 0.25 to 1
- w_gate: bfloat16 [8, 6144, 8192], P('ep', None, 'fsdp'), may hold values from -0.078125 to 0.078125
- w_up: bfloat16 [8, 6144, 8192], P('ep', None, 'fsdp'), may hold values from -0.078125 to 0.078125
- w_down: bfloat16 [8, 8192, 6144], P('ep', 'fsdp'), may hold values from -0.0625 to 0.0625
Outputs:
- mixed_rows: bfloat16 [1024, 6144], P('ep', 'fsdp')
Inputs may be any that keep to these rules, and one draw needn't show every extreme that they name: `expert_ids`: among the 128 tokens of one index of ep (aligned blocks of rows), no expert is named by more than 64 rows, a bound that some block reaches; a token names two different experts.
All inputs are finite; a program needn't handle non-finite values.
Results may differ from a plain program's by a relative error of at most 0.0057.
Values may be sent and summed in bfloat16 or wider, within the bound.
No kernel may reach another device: no remote copies, remote signals or barrier semaphores. Data moves between devices by JAX's collectives and lax.ppermute only.
A program may use at most 128 MiB of HBM per device.

v0:
```python
import jax
import jax.numpy as jnp
from jax import lax
from jax.sharding import PartitionSpec as P


def shards(tokens, expert_ids, combine_weights, w_gate, w_up, w_down):
    groups = lax.axis_size("ep")
    tok_rows = tokens.shape[0]
    width_local = tokens.shape[1]
    capacity = min(tok_rows, 4 * tok_rows // groups)
    experts_all = groups * w_gate.shape[0]
    chosen = expert_ids.reshape(-1)
    expert_lane = jnp.arange(experts_all, dtype=jnp.int32)
    onehot = (chosen[:, None] == expert_lane[None, :]).astype(jnp.int32)
    before = jnp.cumsum(onehot, axis=0, dtype=jnp.int32) - onehot
    slot_index = jnp.sum(before * onehot, axis=1)
    position = (chosen * capacity + slot_index).reshape(tok_rows, 2)
    places = jnp.arange(experts_all * capacity, dtype=jnp.int32)
    select = position[:, :, None] == places[None, None, :]
    dispatch = jnp.sum(select.astype(jnp.float32), axis=1).astype(jnp.bfloat16)
    packed = lax.dot_general(
        dispatch, tokens, (((0,), (0,)), ((), ())), preferred_element_type=jnp.float32
    )
    packed = packed.astype(jnp.bfloat16).reshape(experts_all, capacity, width_local)
    arrived = lax.all_to_all(packed, "ep", split_axis=0, concat_axis=0, tiled=True)
    expert_rows = arrived.reshape(groups * capacity, width_local)
    gate_local = w_gate[0]
    up_local = w_up[0]
    down_local = w_down[0]
    section = lax.all_gather(expert_rows, "fsdp", axis=1, tiled=True)
    gate_sums = jnp.dot(section, gate_local, preferred_element_type=jnp.float32)
    up_sums = jnp.dot(section, up_local, preferred_element_type=jnp.float32)
    hidden = (jax.nn.silu(gate_sums) * up_sums).astype(jnp.bfloat16)
    summed = lax.psum_scatter(
        lax.dot_general(
            down_local, hidden, (((0,), (1,)), ((), ())), preferred_element_type=jnp.float32
        ),
        "fsdp",
        scatter_dimension=0,
        tiled=True,
    )
    result = summed.T.astype(jnp.bfloat16)
    returned = lax.all_to_all(
        result.reshape(groups, capacity, width_local), "ep", split_axis=0, concat_axis=0, tiled=True
    )
    weighting = jnp.sum(jnp.where(select, combine_weights[:, :, None], 0.0), axis=1)
    mixed_rows = jnp.dot(
        weighting,
        returned.reshape(-1, width_local).astype(jnp.float32),
        precision=lax.Precision.HIGHEST,
    )
    return mixed_rows.astype(jnp.bfloat16)


def solution(mesh):
    in_specs = (
        P("ep", "fsdp"),
        P("ep", None),
        P("ep", None),
        P("ep", None, "fsdp"),
        P("ep", None, "fsdp"),
        P("ep", "fsdp", None),
    )
    out_specs = P("ep", "fsdp")
    return jax.shard_map(shards, mesh=mesh, in_specs=in_specs, out_specs=out_specs, check_vma=False)
```

profile of v0, /device:TPU:2, one launch (start us, length us, event | category | flops | bytes accessed | tf_op | source)
XLA Modules:
  0.0 336.2 jit_solution(7917061776976984634)
XLA Ops:
  6.5 0.0 copy-start
  6.5 0.0 all-gather.2.cloned.1.call-start
  6.5 0.9 copy.29
  7.5 0.1 eq.42
  7.6 0.1 eq.38
  7.8 0.6 reduce-window.6
  8.4 0.2 slice_reduce_fusion
  8.6 0.1 fusion.21
  8.7 0.1 reduce_sum.30
  8.9 0.1 copy.31
  8.9 0.7 multiply_add_fusion
  9.6 1.6 convert_reduce_fusion
  11.2 1.7 convolution_convert_fusion
  12.8 1.1 copy.32
  13.9 20.8 %all_to_all.10 = bf16[8,64,192]{2,1,0:T(8,128)(2,1)} all-to-all(bf16[8,64,192]{2,1,0:T(8,128)(2,1)S(1)} %bitcast.38), channel_id=1, replica_groups=mesh['ep'=8,'fsdp'=32] {'ep'}, dimensions={0} | all-to-all | bytes 393216 | tf_op jit(solution)/shard_map/all_to_all | solution.py:26
  34.7 1.8 copy.33
  36.5 0.0 all-gather.2.cloned.1.call-update
  36.5 0.0 reduce-scatter.4.cloned.1.call-start
  36.5 65.6 %all-gather.2.cloned.1.call-done = bf16[512,6144]{0,1:T(8,128)(2,1)} async-done(((bf16[512,192]{0,1:T(8,128)(2,1)}), bf16[512,6144]{0,1:T(8,128)(2,1)}) %all-gather.2.cloned.1.call-update) | async-done | bytes 6291472 | tf_op jit(solution)/shard_map/all_gather | solution.py:31
  102.2 6.3 %fusion.3 = f32[512,256]{1,0:T(8,128)} fusion(bf16[512,6144]{0,1:T(8,128)(2,1)} %all-gather.2.cloned.1.call-done, bf16[1,6144,256]{2,1,0:T(8,128)(2,1)} %param.9), kind=kOutput, calls=%fused_computation.4 | convolution fusion | flops 1610612736 | bytes 9961472 | tf_op jit(solution)/shard_map/dot_general | solution.py:32
  108.5 0.0 copy-done
  108.5 15.0 %convolution_bitcast_fusion = f32[6144,512]{0,1:T(8,128)} fusion(bf16[1,256,6144]{2,1,0:T(8,128)(2,1)S(1)} %copy-done, bf16[512,6144]{0,1:T(8,128)(2,1)} %all-gather.2.cloned.1.call-done, bf16[1,6144,256]{2,1,0:T(8,128)(2,1)} %param.10, f32[512,256]{1,0:T(8,128)} %fusion.3), kind=kOutput, calls=%fused_computation | convolution fusion | flops 3222011904 | bytes 25690112 | tf_op jit(solution)/shard_map/dot_general | solution.py:36
  123.5 12.6 %copy.34 = f32[6144,512]{1,0:T(8,128)} copy(f32[6144,512]{0,1:T(8,128)} %convolution_bitcast_fusion) | data formatting | bytes 25165824
  136.1 0.0 copy-start.1
  136.1 0.0 reduce-scatter.4.cloned.1.call-update
  136.1 174.5 %reduce-scatter.4.cloned.1.call-done = f32[192,512]{1,0:T(8,128)} async-done(((f32[6144,512]{1,0:T(8,128)}), f32[192,512]{1,0:T(8,128)}) %reduce-scatter.4.cloned.1.call-update) | async-done | bytes 393232
  310.6 1.8 copy.35
  312.4 15.9 %all_to_all.11 = bf16[8,64,192]{2,1,0:T(8,128)(2,1)S(1)} all-to-all(bf16[8,64,192]{2,1,0:T(8,128)(2,1)} %bitcast.41), channel_id=1, replica_groups=mesh['ep'=8,'fsdp'=32] {'ep'}, dimensions={0} | all-to-all | bytes 393216 | tf_op jit(solution)/shard_map/all_to_all | solution.py:44
  328.4 0.0 copy-done.1
  328.4 1.0 convolution_convert_fusion.1
  (3 shorter events, 0.0 us)
Async XLA Ops:
  6.5 102.0 %copy-start = (bf16[1,256,6144]{2,1,0:T(8,128)(2,1)S(1)}, bf16[1,256,6144]{2,1,0:T(8,128)(2,1)}, u32[]{:S(2)}) copy-start(bf16[1,256,6144]{2,1,0:T(8,128)(2,1)} %param.11) | copy-start | bytes 9437188
  6.5 95.6 %all-gather.2.cloned.1.call-start = ((), (), s32[]{:S(2)}) async-start(), calls=%async_computation.3 | async-start | bytes 6488064 | tf_op jit(solution)/shard_map/all_gather | solution.py:31
  36.5 274.1 %reduce-scatter.4.cloned.1.call-start = ((), (), s32[]{:S(2)}) async-start(), calls=%async_computation.4 | async-start | bytes 12976128
  136.1 192.3 %copy-start.1 = (f32[128,512]{1,0:T(8,128)S(1)}, f32[128,512]{1,0:T(8,128)}, u32[]{:S(2)}) copy-start(f32[128,512]{1,0:T(8,128)} %get-tuple-element.6) | copy-start | bytes 786436
Sparse Core Ops, SparseCore 0:
  36.6 65.5 all-gather.1
  136.3 174.3 reduce-scatter.3
where the time goes:
time: 337 us; the launch traced here: 336 us
  waiting for transfers between devices  240 us (71%)
  blocking collectives  36.7 us (11%)
  matrix products  24 us (7%)
  local copies, waits for them, and re-layouts  18.9 us (6%)
  between operations  13.4 us (4%)
    unnamed x3, waiting for transfers between devices  175 us
    all_gather x1, waiting for transfers between devices, shards(): section = lax.all_gather(expert_rows, 'fsdp', axis=1, tiled=True)  65.6 us
    all_to_all x1, blocking collectives, shards(): lax.all_to_all(packed, 'ep', split_axis=0, concat_axis=0, tiled=True)  20.8 us
    all_to_all x1, blocking collectives, shards(): lax.all_to_all(result.reshape(groups, capacity, width_local), 'ep', split...  15.9 us
    unnamed x7, local copies, waits for them, and re-layouts  15.4 us
    dot_general x1, matrix products, shards(): lax.dot_general(down_local, hidden, (((0,), (1,)), ((), ())), preferred_e...  15 us
  transfers between devices with their start and end apart: 2, of which 2 were waited for; matrix products, arithmetic and copies ran while one was open for 0% of the time, Pallas kernels for 0%

commit v1 on v0

--- a/solution.py
+++ b/solution.py
@@ -28,7 +28,9 @@
     gate_local = w_gate[0]
     up_local = w_up[0]
     down_local = w_down[0]
-    section = lax.all_gather(expert_rows, "fsdp", axis=1, tiled=True)
+    section = jnp.concatenate(
+        lax.all_to_all(jnp.stack([expert_rows] * lax.axis_size("fsdp")), "fsdp", 0, 0), axis=1
+    )
     gate_sums = jnp.dot(section, gate_local, preferred_element_type=jnp.float32)
     up_sums = jnp.dot(section, up_local, preferred_element_type=jnp.float32)
     hidden = (jax.nn.silu(gate_sums) * up_sums).astype(jnp.bfloat16)

time: 337 us -> 414 us (1.23)
  blocking collectives: 36.7 us -> 187 us
  waiting for transfers between devices: 240 us -> 168 us
    all_to_all x0 -> x1, blocking collectives: none -> 149 us  [shards(): lax.all_to_all(jnp.stack([expert_rows] * lax.axis_size('fsdp')), 'fsdp',...]
    all_gather x1 -> x0, waiting for transfers between devices: 65.6 us -> none  [shards(): section = lax.all_gather(expert_rows, 'fsdp', axis=1, tiled=True)]
    unnamed x3 -> x2, waiting for transfers between devices: 175 us -> 168 us
    unnamed x7 -> x11, local copies, waits for them, and re-layouts: 15.4 us -> 18 us
  transfers between devices with their start and end apart: 2 -> 1, of which waited for: 2 -> 1; matrix products, arithmetic and copies ran while one was open for 0% -> 0% of each run, Pallas kernels for 0% -> 0%
where the time goes in v1:
time: 414 us
  blocking collectives  187 us (45%)
  waiting for transfers between devices  168 us (41%)
  local copies, waits for them, and re-layouts  21.5 us (5%)
  matrix products  20.3 us (5%)
  between operations  13.5 us (3%)
    unnamed x2, waiting for transfers between devices  168 us
    all_to_all x1, blocking collectives, shards(): lax.all_to_all(jnp.stack([expert_rows] * lax.axis_size('fsdp')), 'fsdp',...  149 us
    all_to_all x1, blocking collectives, shards(): lax.all_to_all(packed, 'ep', split_axis=0, concat_axis=0, tiled=True)  20.8 us
    unnamed x11, local copies, waits for them, and re-layouts  18 us
    all_to_all x1, blocking collectives, shards(): lax.all_to_all(result.reshape(groups, capacity, width_local), 'ep', split...  17.2 us
    dot_general x1, matrix products, shards(): lax.dot_general(down_local, hidden, (((0,), (1,)), ((), ())), preferred_e...  15 us
  transfers between devices with their start and end apart: 1, of which 1 were waited for; matrix products, arithmetic and copies ran while one was open for 0% of the time, Pallas kernels for 0%

profile of v1, /device:TPU:2, one launch (start us, length us, event | category | flops | bytes accessed | tf_op | source)
XLA Modules:
  0.0 413.6 jit_solution(5786549004810088262)
XLA Ops:
  6.5 0.0 copy-start
  6.5 0.0 reduce-scatter.4.cloned.1.call-start
  6.5 0.9 copy.31
  7.5 0.1 eq.42
  7.6 0.1 eq.38
  7.8 0.6 reduce-window.6
  8.4 0.2 slice_reduce_fusion
  8.6 0.1 fusion.21
  8.7 0.1 reduce_sum.30
  8.9 0.1 copy.33
  8.9 0.7 multiply_add_fusion
  9.6 1.6 convert_reduce_fusion
  11.2 1.7 convolution_convert_fusion
  12.8 1.1 copy.34
  13.9 20.8 %all_to_all.15 = bf16[8,64,192]{2,1,0:T(8,128)(2,1)} all-to-all(bf16[8,64,192]{2,1,0:T(8,128)(2,1)S(1)} %bitcast.43), channel_id=1, replica_groups=mesh['ep'=8,'fsdp'=32] {'ep'}, dimensions={0} | all-to-all | bytes 393216 | tf_op jit(solution)/shard_map/all_to_all | solution.py:26
  34.7 1.1 copy.35
  35.8 0.7 stack.3
  36.5 0.0 copy-start.2
  36.5 148.8 %all_to_all.16 = bf16[32,512,192]{1,2,0:T(8,128)(2,1)S(1)} all-to-all(bf16[32,512,192]{1,2,0:T(8,128)(2,1)S(1)} %stack.3), channel_id=1, replica_groups=mesh['ep'=8,'fsdp'=32] {'fsdp'}, dimensions={0} | all-to-all | bytes 12582912 | tf_op jit(solution)/shard_map/all_to_all | solution.py:32
  185.3 0.0 copy-start.1
  185.3 2.6 copy-done.1
  188.0 0.0 copy-done.2
  188.0 2.6 fusion.3
  190.6 0.0 copy-done
  190.6 15.0 %convolution_bitcast_fusion = f32[6144,512]{0,1:T(8,128)} fusion(bf16[1,256,6144]{2,1,0:T(8,128)(2,1)S(1)} %copy-done, bf16[512,6144]{0,1:T(8,128)(2,1)} %bitcast.42, bf16[1,6144,256]{2,1,0:T(8,128)(2,1)} %param.10, f32[512,256]{1,0:T(8,128)} %fusion.3), kind=kOutput, calls=%fused_computation | convolution fusion | flops 3222011904 | bytes 25690112 | tf_op jit(solution)/shard_map/dot_general | solution.py:38
  205.6 12.6 %copy.36 = f32[6144,512]{1,0:T(8,128)} copy(f32[6144,512]{0,1:T(8,128)} %convolution_bitcast_fusion) | data formatting | bytes 25165824
  218.2 0.0 copy-start.3
  218.2 0.0 reduce-scatter.4.cloned.1.call-update
  218.2 168.5 %reduce-scatter.4.cloned.1.call-done = f32[192,512]{1,0:T(8,128)} async-done(((f32[6144,512]{1,0:T(8,128)}), f32[192,512]{1,0:T(8,128)}) %reduce-scatter.4.cloned.1.call-update) | async-done | bytes 393232
  386.7 1.8 copy.37
  388.5 17.2 %all_to_all.17 = bf16[8,64,192]{2,1,0:T(8,128)(2,1)S(1)} all-to-all(bf16[8,64,192]{2,1,0:T(8,128)(2,1)} %bitcast.46), channel_id=1, replica_groups=mesh['ep'=8,'fsdp'=32] {'ep'}, dimensions={0} | all-to-all | bytes 393216 | tf_op jit(solution)/shard_map/all_to_all | solution.py:46
  405.7 0.0 copy-done.3
  405.7 1.0 convolution_convert_fusion.1
  (3 shorter events, 0.0 us)
Async XLA Ops:
  6.5 184.0 %copy-start = (bf16[1,256,6144]{2,1,0:T(8,128)(2,1)S(1)}, bf16[1,256,6144]{2,1,0:T(8,128)(2,1)}, u32[]{:S(2)}) copy-start(bf16[1,256,6144]{2,1,0:T(8,128)(2,1)} %param.11) | copy-start | bytes 9437188
  6.5 380.2 %reduce-scatter.4.cloned.1.call-start = ((), (), s32[]{:S(2)}) async-start(), calls=%async_computation.4 | async-start | bytes 12976128
  36.5 151.5 %copy-start.2 = (bf16[1,6144,256]{2,1,0:T(8,128)(2,1)S(1)}, bf16[1,6144,256]{2,1,0:T(8,128)(2,1)}, u32[]{:S(2)}) copy-start(bf16[1,6144,256]{2,1,0:T(8,128)(2,1)} %param.9) | copy-start | bytes 9437188
  185.3 2.6 copy-start.1
  218.2 187.5 %copy-start.3 = (f32[128,512]{1,0:T(8,128)S(1)}, f32[128,512]{1,0:T(8,128)}, u32[]{:S(2)}) copy-start(f32[128,512]{1,0:T(8,128)} %get-tuple-element.6) | copy-start | bytes 786436
Sparse Core Ops, SparseCore 0:
  218.3 168.3 reduce-scatter.3
